TPU v7x, 32 devices: a whole 2x2x4 slice. The times are simulated.
32 devices in a mesh: gx: 8 (over y, x, core), gy: 4 (over z).
Axes of the slice: x: 2, y: 2, z: 4, core: 2. Of those that a mesh axis runs over, the one named last changes fastest.
Arguments:
- provisional: bfloat16 [4, 8, 1024, 1024], P(None, 'gx', 'gy'), may hold values from -6 to 6
- implicit_terms: bfloat16 [4, 8, 1024, 1024], P(None, 'gx', 'gy'), may hold values from -6 to 6
- adv_speed: float32 [8, 1024], P('gx'), may hold values from 0.2 to 1.2
- reaction: float32 [8, 1024], P('gx'), may hold values from 0.1 to 2
- wall_rate: float32 [1024], replicated, may hold values from 0.05 to 20
- span_rate: float32 [1024], replicated, may hold values from 0.01 to 4
- analysis: bfloat16 [1024, 1024], replicated, may hold values from -1 to 2
- synthesis: bfloat16 [1024, 1024], replicated, may hold values from -1 to 2
Outputs:
- end_value: float32 [8, 1024, 1024], P('gx', 'gy')
All inputs are finite; a program needn't handle non-finite values.
Results may differ from a plain program's by a relative error of at most 0.0063.
Values may be sent and summed in bfloat16 or wider, within the bound.
A program may use at most 64 MiB of HBM per device.

v0:
```python
import math
import jax
import jax.numpy as jnp
from jax import lax
from jax.sharding import PartitionSpec as P


def spectral_weights():
    root_five = math.sqrt(5.0)
    points = [0.0, 0.5 - 0.5 / root_five, 0.5 + 0.5 / root_five, 1.0]
    gauss_offset = 1.0 / math.sqrt(3.0)
    weights = [[0.0, 0.0, 0.0, 0.0] for m in range(3)]
    for m in range(3):
        half_width = 0.5 * (points[m + 1] - points[m])
        centre = 0.5 * (points[m + 1] + points[m])
        for sign_factor in (-1.0, 1.0):
            sample = centre + half_width * sign_factor * gauss_offset
            for j in range(4):
                basis_value = 1.0
                for i in range(4):
                    if i != j:
                        basis_value = basis_value * (sample - points[i]) / (points[j] - points[i])
                weights[m][j] = weights[m][j] + half_width * basis_value
    return (points, weights)


def shifted(cells, axis):
    count = lax.axis_size(axis)
    behind = lax.ppermute(cells, axis, [(i, (i + 1) % count) for i in range(count)])
    forward = lax.ppermute(cells, axis, [((i + 1) % count, i) for i in range(count)])
    return forward.astype(jnp.float32) - behind.astype(jnp.float32)


def per_device(
    provisional, implicit_terms, adv_speed, reaction, wall_rate, span_rate, analysis, synthesis
):
    points, weights = spectral_weights()
    steps = [float(points[m + 1] - points[m]) for m in range(3)]
    modes_dev = span_rate.shape[0] // lax.axis_size("gy")
    span_part = lax.dynamic_slice_in_dim(span_rate, lax.axis_index("gy") * modes_dev, modes_dev, 0)
    rows_dev = provisional.shape[2]
    row_start = lax.axis_index("gy") * rows_dev
    half_speed = 0.5 * adv_speed[0][:, None]
    decay = reaction[0][:, None]
    half_speed_part = lax.dynamic_slice_in_dim(half_speed, row_start, rows_dev, 0)
    decay_part = lax.dynamic_slice_in_dim(decay, row_start, rows_dev, 0)
    prov = [provisional[j, 0].astype(jnp.float32) for j in range(4)]
    impl = [implicit_terms[j, 0].astype(jnp.float32) for j in range(4)]
    known = []
    for m in range(3):
        field_weights = [weights[m][j] - (steps[m] if m == j and m > 0 else 0.0) for j in range(4)]
        impl_weights = [weights[m][j] - (steps[m] if j == m + 1 else 0.0) for j in range(4)]
        mixed = sum((float(field_weights[j]) * prov[j] for j in range(4)))
        local = sum((float(impl_weights[j]) * impl[j] for j in range(4))) - decay_part * mixed
        if m == 0:
            local = local + prov[0]
        local = local - half_speed_part * shifted(mixed.astype(jnp.bfloat16), "gx")
        known.append(local.astype(jnp.bfloat16))
    known = [
        lax.all_to_all(field, "gy", split_axis=1, concat_axis=0, tiled=True) for field in known
    ]
    for m in range(3):
        rhs = known[m].astype(jnp.float32)
        if m:
            sent = current.astype(jnp.bfloat16)
            rhs = (
                rhs
                + current
                - steps[m] * (decay * sent.astype(jnp.float32) + half_speed * shifted(sent, "gx"))
            )
        factors = 1.0 / (1.0 + steps[m] * (wall_rate[:, None] + span_part[None, :]))
        coefficients = jnp.dot(
            analysis, rhs.astype(jnp.bfloat16), preferred_element_type=jnp.float32
        )
        scaled = (coefficients * factors).astype(jnp.bfloat16)
        current = jnp.dot(synthesis, scaled, preferred_element_type=jnp.float32)
    result = lax.all_to_all(
        current.astype(jnp.bfloat16), "gy", split_axis=0, concat_axis=1, tiled=True
    )
    return result.astype(jnp.float32)[None]


def solution(mesh):
    placed = (
        P(None, "gx", "gy", None),
        P(None, "gx", "gy", None),
        P("gx", None),
        P("gx", None),
        P(),
        P(),
        P(),
        P(),
    )
    return jax.shard_map(
        per_device, mesh=mesh, in_specs=placed, out_specs=P("gx", "gy", None), check_vma=False
    )
```

profile of v0, /device:TPU:3, one launch (start us, length us, event | category | flops | bytes accessed | tf_op | source)
XLA Modules:
  0.0 144.3 jit_solution(17562041078309248272)
XLA Ops:
  0.0 2.8 %fusion.85 = (bf16[1,1,256,1024]{3,2,1,0:T(8,128)(2,1)S(1)}, bf16[1,1,256,1024]{3,2,1,0:T(8,128)(2,1)}, bf16[1,1,256,1024]{3,2,1,0:T(8,128)(2,1)}, bf16[1,1,256,1024]{3,2,1,0:T(8,128)(2,1)}) fusion(bf16[4,1,256,1024]{3,2,1,0:T(8,128)(2,1)} %param.8), kind=kLoop, calls=%fused_computation.115 | loop fusion | bytes 4194304 | tf_op jit(solution)/shard_map/slice | solution.py:47
  2.8 0.2 copy.44
  3.0 1.2 copy.45
  4.3 2.1 %copy.46 = bf16[1,1,256,1024]{2,3,1,0:T(8,128)(2,1)} copy(bf16[1,1,256,1024]{3,2,1,0:T(8,128)(2,1)} %get-tuple-element.12) | data formatting | bytes 1048576
  6.4 2.1 %copy.47 = bf16[1,1,256,1024]{2,3,1,0:T(8,128)(2,1)} copy(bf16[1,1,256,1024]{3,2,1,0:T(8,128)(2,1)} %get-tuple-element.14) | data formatting | bytes 1048576
  8.4 3.1 %fusion.76 = (bf16[256,1024]{0,1:T(8,128)(2,1)}, bf16[256,1024]{0,1:T(8,128)(2,1)}, bf16[256,1024]{0,1:T(8,128)(2,1)}) fusion(bf16[1,1,256,1024]{2,3,1,0:T(8,128)(2,1)} %copy.47, bf16[1,1,256,1024]{2,3,1,0:T(8,128)(2,1)} %copy.46, bf16[1,1,256,1024]{2,3,1,0:T(8,128)(2,1)S(1)} %copy.45, bf16[1,1,256,1024]{2,3,1,0:T(8,128)(2,1)S(1)} %copy.44), kind=kLoop, calls=%fused_computation.105 | loop fusion | flops 7340032 | bytes 3670016 | tf_op jit(solution)/shard_map/convert_element_type | solution.py:57
  11.6 0.7 collective-permute-start
  12.2 2.0 %collective-permute-start.1 = (bf16[256,1024]{0,1:T(8,128)(2,1)}, bf16[256,1024]{0,1:T(8,128)(2,1)}, u32[]{:S(2)}, u32[]{:S(2)}) collective-permute-start(bf16[256,1024]{0,1:T(8,128)(2,1)} %get-tuple-element.8), channel_id=1, source_target_pairs={{0,4},{4,8},{8,12},{12,16},{16,20},{20,24},{24,28},{28,0},{1,5},{5... | collective-permute-start | bytes 1572872 | tf_op jit(solution)/shard_map/ppermute | solution.py:29
  14.2 2.6 %collective-permute-start.3 = (bf16[256,1024]{0,1:T(8,128)(2,1)}, bf16[256,1024]{0,1:T(8,128)(2,1)}, u32[]{:S(2)}, u32[]{:S(2)}) collective-permute-start(bf16[256,1024]{0,1:T(8,128)(2,1)} %get-tuple-element.9), channel_id=1, source_target_pairs={{0,4},{4,8},{8,12},{12,16},{16,20},{20,24},{24,28},{28,0},{1,5},{5... | collective-permute-start | bytes 1572872 | tf_op jit(solution)/shard_map/ppermute | solution.py:29
  16.8 0.0 collective-permute-start.4
  16.9 10.1 %collective-permute-done = bf16[256,1024]{0,1:T(8,128)(2,1)} collective-permute-done((bf16[256,1024]{0,1:T(8,128)(2,1)}, bf16[256,1024]{0,1:T(8,128)(2,1)}, u32[]{:S(2)}, u32[]{:S(2)}) %collective-permute-start) | collective-permute-done | bytes 524320 | tf_op jit(solution)/shard_map/ppermute | solution.py:30
  26.9 0.0 collective-permute-start.5
  26.9 2.9 %fusion.86 = (bf16[1,1,256,1024]{3,2,1,0:T(8,128)(2,1)}, bf16[1,1,256,1024]{3,2,1,0:T(8,128)(2,1)}, bf16[1,1,256,1024]{3,2,1,0:T(8,128)(2,1)}, bf16[1,1,256,1024]{3,2,1,0:T(8,128)(2,1)}) fusion(bf16[4,1,256,1024]{3,2,1,0:T(8,128)(2,1)} %param.9), kind=kLoop, calls=%fused_computation.116 | loop fusion | bytes 4194304 | tf_op jit(solution)/shard_map/slice | solution.py:48
  29.8 2.1 %copy.40 = bf16[1,1,256,1024]{2,3,1,0:T(8,128)(2,1)} copy(bf16[1,1,256,1024]{3,2,1,0:T(8,128)(2,1)} %get-tuple-element.15) | data formatting | bytes 1048576
  31.9 2.0 %copy.41 = bf16[1,1,256,1024]{2,3,1,0:T(8,128)(2,1)} copy(bf16[1,1,256,1024]{3,2,1,0:T(8,128)(2,1)} %get-tuple-element.17) | data formatting | bytes 1048576
  33.9 2.0 %copy.42 = bf16[1,1,256,1024]{2,3,1,0:T(8,128)(2,1)} copy(bf16[1,1,256,1024]{3,2,1,0:T(8,128)(2,1)} %get-tuple-element.16) | data formatting | bytes 1048576
  36.0 2.1 %copy.43 = bf16[1,1,256,1024]{2,3,1,0:T(8,128)(2,1)} copy(bf16[1,1,256,1024]{3,2,1,0:T(8,128)(2,1)} %get-tuple-element.18) | data formatting | bytes 1048576
  38.1 0.0 collective-permute-done.1
  38.1 0.1 collective-permute-done.2
  38.2 0.0 collective-permute-done.3
  38.2 11.2 %collective-permute-done.4 = bf16[256,1024]{0,1:T(8,128)(2,1)} collective-permute-done((bf16[256,1024]{0,1:T(8,128)(2,1)}, bf16[256,1024]{0,1:T(8,128)(2,1)}, u32[]{:S(2)}, u32[]{:S(2)}) %collective-permute-start.4) | collective-permute-done | bytes 524320 | tf_op jit(solution)/shard_map/ppermute | solution.py:30
  49.4 0.0 collective-permute-done.5
  49.4 5.2 %fusion.17 = (bf16[256,1024]{0,1:T(8,128)(2,1)}, bf16[256,1024]{0,1:T(8,128)(2,1)}, bf16[256,1024]{0,1:T(8,128)(2,1)S(1)}) fusion(bf16[1,1,256,1024]{2,3,1,0:T(8,128)(2,1)} %copy.40, bf16[1,1,256,1024]{2,3,1,0:T(8,128)(2,1)} %copy.41, bf16[1,1,256,1024]{2,3,1,0:T(8,128)(2,1)} %copy.42, bf16[1,1,256,1024]{2,3,1,0:T(8,128)(2,1)} %copy.43, ...), kind=kLoop, calls=%fused_computation.49 | loop fusion | flops 19660800 | bytes 8914944 | tf_op jit(solution)/shard_map/convert_element_type | solution.py:58
  54.7 0.0 copy-start.3
  54.7 18.7 %all_to_all.58 = bf16[256,4,256]{0,2,1:T(8,128)(2,1)S(1)} all-to-all(bf16[256,4,256]{0,2,1:T(8,128)(2,1)S(1)} %bitcast.194), channel_id=1, replica_groups=mesh['gx'=8,'gy'=4] {'gy'}, dimensions={1} | all-to-all | bytes 1048576 | tf_op jit(solution)/shard_map/all_to_all | solution.py:60
  73.4 3.5 %all-to-all-start.1 = ((bf16[256,4,256]{0,2,1:T(8,128)(2,1)}), bf16[256,4,256]{0,2,1:T(8,128)(2,1)S(1)}, u32[]{:S(2)}, u32[]{:S(2)}) async-start(bf16[256,4,256]{0,2,1:T(8,128)(2,1)} %bitcast.193), calls=%async_computation.1 | async-start | bytes 1048576 | tf_op jit(solution)/shard_map/all_to_all | solution.py:60
  76.9 0.8 dynamic_slice.11
  77.7 1.0 copy.37
  78.7 4.3 %fusion.87 = (bf16[1024,256]{0,1:T(8,128)(2,1)}, f32[1024,256]{0,1:T(8,128)}) fusion(bf16[1024,1024]{1,0:T(8,128)(2,1)S(1)} %copy-done, bf16[1024,256]{1,0:T(8,128)(2,1)} %bitcast.200, bf16[1024,1024]{1,0:T(8,128)(2,1)} %param.14, f32[256]{0:T(256)S(1)} %dynamic_slice.11, f32[1024]{0:T(1024)S(1)} %copy-done.3), kind=kOutput, calls=%fused_computation.117 | convolution fusion | flops 1075576832 | bytes 6296576 | tf_op jit(solution)/shard_map/dot_general | solution.py:76
  83.0 0.4 collective-permute-start.6
  83.4 2.3 %collective-permute-start.7 = (bf16[1024,256]{0,1:T(8,128)(2,1)}, bf16[1024,256]{0,1:T(8,128)(2,1)}, u32[]{:S(2)}, u32[]{:S(2)}) collective-permute-start(bf16[1024,256]{0,1:T(8,128)(2,1)} %get-tuple-element.19), channel_id=1, source_target_pairs={{0,4},{4,8},{8,12},{12,16},{16,20},{20,24},{24,28},{28,0},{1,5},{5... | collective-permute-start | bytes 1572872 | tf_op jit(solution)/shard_map/ppermute | solution.py:29
  85.7 5.4 %all-to-all-done.1 = bf16[256,4,256]{0,2,1:T(8,128)(2,1)S(1)} async-done(((bf16[256,4,256]{0,2,1:T(8,128)(2,1)}), bf16[256,4,256]{0,2,1:T(8,128)(2,1)S(1)}, u32[]{:S(2)}, u32[]{:S(2)}) %all-to-all-start.1) | async-done | bytes 524320 | tf_op jit(solution)/shard_map/all_to_all | solution.py:60
  91.1 3.5 %all-to-all-start = ((bf16[256,4,256]{0,2,1:T(8,128)(2,1)}), bf16[256,4,256]{0,2,1:T(8,128)(2,1)S(1)}, u32[]{:S(2)}, u32[]{:S(2)}) async-start(bf16[256,4,256]{0,2,1:T(8,128)(2,1)} %bitcast.7), calls=%async_computation | async-start | bytes 1048576 | tf_op jit(solution)/shard_map/all_to_all | solution.py:60
  94.6 0.1 convert_bitcast_fusion
  94.7 1.1 copy.50
  95.8 2.2 %collective-permute-done.6 = bf16[1024,256]{0,1:T(8,128)(2,1)} collective-permute-done((bf16[1024,256]{0,1:T(8,128)(2,1)}, bf16[1024,256]{0,1:T(8,128)(2,1)}, u32[]{:S(2)}, u32[]{:S(2)}) %collective-permute-start.6) | collective-permute-done | bytes 524320 | tf_op jit(solution)/shard_map/ppermute | solution.py:30
  98.0 5.3 %fusion.88 = (bf16[1024,256]{0,1:T(8,128)(2,1)}, f32[1024,256]{0,1:T(8,128)}) fusion(bf16[1024,1024]{1,0:T(8,128)(2,1)S(1)} %copy-done, bf16[1024,1024]{1,0:T(8,128)(2,1)} %param.14, bf16[1024,256]{0,1:T(8,128)(2,1)} %collective-permute-done.7, bf16[1024,256]{0,1:T(8,128)(2,1)} %collective-permute-done.6, bf16[1024,256]{0,1:T(8,128)(2,1)} %get-tuple-element.19, ...), kind=kOutput, calls=%fused_computation.118 | convolution fusion | flops 1078460416 | bytes 9450496 | tf_op jit(solution)/shard_map/dot_general | solution.py:76
  103.3 0.0 collective-permute-start.8
  103.3 2.6 %collective-permute-start.9 = (bf16[1024,256]{0,1:T(8,128)(2,1)}, bf16[1024,256]{0,1:T(8,128)(2,1)}, u32[]{:S(2)}, u32[]{:S(2)}) collective-permute-start(bf16[1024,256]{0,1:T(8,128)(2,1)} %get-tuple-element.21), channel_id=1, source_target_pairs={{0,4},{4,8},{8,12},{12,16},{16,20},{20,24},{24,28},{28,0},{1,5},{5... | collective-permute-start | bytes 1572872 | tf_op jit(solution)/shard_map/ppermute | solution.py:29
  106.0 2.6 %all-to-all-done = bf16[256,4,256]{0,2,1:T(8,128)(2,1)S(1)} async-done(((bf16[256,4,256]{0,2,1:T(8,128)(2,1)}), bf16[256,4,256]{0,2,1:T(8,128)(2,1)S(1)}, u32[]{:S(2)}, u32[]{:S(2)}) %all-to-all-start) | async-done | bytes 524320 | tf_op jit(solution)/shard_map/all_to_all | solution.py:60
  108.5 0.1 convert_bitcast_fusion.1
  108.6 0.1 copy.49
  108.8 8.8 %collective-permute-done.8 = bf16[1024,256]{0,1:T(8,128)(2,1)} collective-permute-done((bf16[1024,256]{0,1:T(8,128)(2,1)}, bf16[1024,256]{0,1:T(8,128)(2,1)}, u32[]{:S(2)}, u32[]{:S(2)}) %collective-permute-start.8) | collective-permute-done | bytes 524320 | tf_op jit(solution)/shard_map/ppermute | solution.py:30
  117.6 4.6 %convolution_convert_fusion = bf16[256,1024]{1,0:T(8,128)(2,1)} fusion(bf16[1024,1024]{1,0:T(8,128)(2,1)S(1)} %copy-done, bf16[1024,1024]{1,0:T(8,128)(2,1)} %param.14, bf16[1024,256]{0,1:T(8,128)(2,1)} %collective-permute-done.9, bf16[1024,256]{0,1:T(8,128)(2,1)} %collective-permute-done.8, bf16[1024,256]{0,1:T(8,128)(2,1)} %get-tuple-element.21, ...), kind=kOutput, calls=%fused_computation.35 | convolution fusion | flops 1078460416 | bytes 8401920 | tf_op jit(solution)/shard_map/dot_general | solution.py:76
  122.2 1.1 copy.52
  123.3 19.6 %all_to_all.59 = bf16[4,256,256]{1,2,0:T(8,128)(2,1)S(1)} all-to-all(bf16[4,256,256]{1,2,0:T(8,128)(2,1)S(1)} %bitcast.196), channel_id=1, replica_groups=mesh['gx'=8,'gy'=4] {'gy'}, dimensions={0} | all-to-all | bytes 1048576 | tf_op jit(solution)/shard_map/all_to_all | solution.py:77
  142.9 0.1 convert_element_type.202
  143.0 1.3 copy.39
  (12 shorter events, 0.0 us)
Async XLA Ops:
  0.0 78.7 %copy-start = (bf16[1024,1024]{1,0:T(8,128)(2,1)S(1)}, bf16[1024,1024]{1,0:T(8,128)(2,1)}, u32[]{:S(2)}) copy-start(bf16[1024,1024]{1,0:T(8,128)(2,1)} %param.15) | copy-start | bytes 6291460
  11.6 15.4 %collective-permute-start = (bf16[256,1024]{0,1:T(8,128)(2,1)}, bf16[256,1024]{0,1:T(8,128)(2,1)}, u32[]{:S(2)}, u32[]{:S(2)}) collective-permute-start(bf16[256,1024]{0,1:T(8,128)(2,1)} %get-tuple-element.8), channel_id=1, source_target_pairs={{4,0},{8,4},{12,8},{16,12},{20,16},{24,20},{28,24},{0,28},{5,1},{9... | collective-permute-start | bytes 1572872 | tf_op jit(solution)/shard_map/ppermute | solution.py:30
  12.2 25.8 %collective-permute-start.1 = (bf16[256,1024]{0,1:T(8,128)(2,1)}, bf16[256,1024]{0,1:T(8,128)(2,1)}, u32[]{:S(2)}, u32[]{:S(2)}) collective-permute-start(bf16[256,1024]{0,1:T(8,128)(2,1)} %get-tuple-element.8), channel_id=1, source_target_pairs={{0,4},{4,8},{8,12},{12,16},{16,20},{20,24},{24,28},{28,0},{1,5},{5... | collective-permute-start | bytes 1572872 | tf_op jit(solution)/shard_map/ppermute | solution.py:29
  14.2 24.0 %collective-permute-start.2 = (bf16[256,1024]{0,1:T(8,128)(2,1)}, bf16[256,1024]{0,1:T(8,128)(2,1)}, u32[]{:S(2)}, u32[]{:S(2)}) collective-permute-start(bf16[256,1024]{0,1:T(8,128)(2,1)} %get-tuple-element.9), channel_id=1, source_target_pairs={{4,0},{8,4},{12,8},{16,12},{20,16},{24,20},{28,24},{0,28},{5,1},{9... | collective-permute-start | bytes 1572872 | tf_op jit(solution)/shard_map/ppermute | solution.py:30
  14.2 24.0 %collective-permute-start.3 = (bf16[256,1024]{0,1:T(8,128)(2,1)}, bf16[256,1024]{0,1:T(8,128)(2,1)}, u32[]{:S(2)}, u32[]{:S(2)}) collective-permute-start(bf16[256,1024]{0,1:T(8,128)(2,1)} %get-tuple-element.9), channel_id=1, source_target_pairs={{0,4},{4,8},{8,12},{12,16},{16,20},{20,24},{24,28},{28,0},{1,5},{5... | collective-permute-start | bytes 1572872 | tf_op jit(solution)/shard_map/ppermute | solution.py:29
  16.8 32.6 %collective-permute-start.4 = (bf16[256,1024]{0,1:T(8,128)(2,1)}, bf16[256,1024]{0,1:T(8,128)(2,1)}, u32[]{:S(2)}, u32[]{:S(2)}) collective-permute-start(bf16[256,1024]{0,1:T(8,128)(2,1)} %get-tuple-element.10), channel_id=1, source_target_pairs={{4,0},{8,4},{12,8},{16,12},{20,16},{24,20},{28,24},{0,28},{5,1},{9... | collective-permute-start | bytes 1572872 | tf_op jit(solution)/shard_map/ppermute | solution.py:30
  26.9 22.5 %collective-permute-start.5 = (bf16[256,1024]{0,1:T(8,128)(2,1)}, bf16[256,1024]{0,1:T(8,128)(2,1)}, u32[]{:S(2)}, u32[]{:S(2)}) collective-permute-start(bf16[256,1024]{0,1:T(8,128)(2,1)} %get-tuple-element.10), channel_id=1, source_target_pairs={{0,4},{4,8},{8,12},{12,16},{16,20},{20,24},{24,28},{28,0},{1,5},{5... | collective-permute-start | bytes 1572872 | tf_op jit(solution)/shard_map/ppermute | solution.py:29
  29.8 8.2 %copy-start.1 = (f32[1,1024]{1,0:T(1,128)S(1)}, f32[1,1024]{1,0:T(1,128)}, u32[]{:S(2)}) copy-start(f32[1,1024]{1,0:T(1,128)} %param.10) | copy-start | bytes 12292
  29.8 8.2 %copy-start.2 = (f32[1,1024]{1,0:T(1,128)S(1)}, f32[1,1024]{1,0:T(1,128)}, u32[]{:S(2)}) copy-start(f32[1,1024]{1,0:T(1,128)} %param.11) | copy-start | bytes 12292
  54.7 24.0 %copy-start.3 = (f32[1024]{0:T(1024)S(1)}, f32[1024]{0:T(1024)}, u32[]{:S(2)}) copy-start(f32[1024]{0:T(1024)} %param.12) | copy-start | bytes 12292
  73.4 17.7 %all-to-all-start.1 = ((bf16[256,4,256]{0,2,1:T(8,128)(2,1)}), bf16[256,4,256]{0,2,1:T(8,128)(2,1)S(1)}, u32[]{:S(2)}, u32[]{:S(2)}) async-start(bf16[256,4,256]{0,2,1:T(8,128)(2,1)} %bitcast.193), calls=%async_computation.1 | async-start | bytes 1048576 | tf_op jit(solution)/shard_map/all_to_all | solution.py:60
  83.0 15.0 %collective-permute-start.6 = (bf16[1024,256]{0,1:T(8,128)(2,1)}, bf16[1024,256]{0,1:T(8,128)(2,1)}, u32[]{:S(2)}, u32[]{:S(2)}) collective-permute-start(bf16[1024,256]{0,1:T(8,128)(2,1)} %get-tuple-element.19), channel_id=1, source_target_pairs={{4,0},{8,4},{12,8},{16,12},{20,16},{24,20},{28,24},{0,28},{5,1},{9... | collective-permute-start | bytes 1572872 | tf_op jit(solution)/shard_map/ppermute | solution.py:30
  83.4 14.6 %collective-permute-start.7 = (bf16[1024,256]{0,1:T(8,128)(2,1)}, bf16[1024,256]{0,1:T(8,128)(2,1)}, u32[]{:S(2)}, u32[]{:S(2)}) collective-permute-start(bf16[1024,256]{0,1:T(8,128)(2,1)} %get-tuple-element.19), channel_id=1, source_target_pairs={{0,4},{4,8},{8,12},{12,16},{16,20},{20,24},{24,28},{28,0},{1,5},{5... | collective-permute-start | bytes 1572872 | tf_op jit(solution)/shard_map/ppermute | solution.py:29
  91.1 17.4 %all-to-all-start = ((bf16[256,4,256]{0,2,1:T(8,128)(2,1)}), bf16[256,4,256]{0,2,1:T(8,128)(2,1)S(1)}, u32[]{:S(2)}, u32[]{:S(2)}) async-start(bf16[256,4,256]{0,2,1:T(8,128)(2,1)} %bitcast.7), calls=%async_computation | async-start | bytes 1048576 | tf_op jit(solution)/shard_map/all_to_all | solution.py:60
  103.3 14.3 %collective-permute-start.8 = (bf16[1024,256]{0,1:T(8,128)(2,1)}, bf16[1024,256]{0,1:T(8,128)(2,1)}, u32[]{:S(2)}, u32[]{:S(2)}) collective-permute-start(bf16[1024,256]{0,1:T(8,128)(2,1)} %get-tuple-element.21), channel_id=1, source_target_pairs={{4,0},{8,4},{12,8},{16,12},{20,16},{24,20},{28,24},{0,28},{5,1},{9... | collective-permute-start | bytes 1572872 | tf_op jit(solution)/shard_map/ppermute | solution.py:30
  103.3 14.3 %collective-permute-start.9 = (bf16[1024,256]{0,1:T(8,128)(2,1)}, bf16[1024,256]{0,1:T(8,128)(2,1)}, u32[]{:S(2)}, u32[]{:S(2)}) collective-permute-start(bf16[1024,256]{0,1:T(8,128)(2,1)} %get-tuple-element.21), channel_id=1, source_target_pairs={{0,4},{4,8},{8,12},{12,16},{16,20},{20,24},{24,28},{28,0},{1,5},{5... | collective-permute-start | bytes 1572872 | tf_op jit(solution)/shard_map/ppermute | solution.py:29
where the time goes:
time: 145 us; the launch traced here: 144 us
  waiting for transfers between devices  40.5 us (28%)
  blocking collectives  38.4 us (26%)
  local copies, waits for them, and re-layouts  24.9 us (17%)
  starting transfers between devices  17.5 us (12%)
  matrix products  14.2 us (10%)
  other arithmetic  8.64 us (6%)
    ppermute x5, waiting for transfers between devices, shifted(): lax.ppermute(cells, axis, [((i + 1) % count, i) for i in range(count)])  32.5 us
    all_to_all x1, blocking collectives, per_device(): lax.all_to_all(current.astype(jnp.bfloat16), 'gy', split_axis=0, concat_a...  19.6 us
    all_to_all x1, blocking collectives, per_device(): lax.all_to_all(field, 'gy', split_axis=1, concat_axis=0, tiled=True)  18.7 us
    dot_general x3, matrix products, per_device(): current = jnp.dot(synthesis, scaled, preferred_element_type=jnp.float32)  14.2 us
    unnamed x16, local copies, waits for them, and re-layouts  13.8 us
    ppermute x5, starting transfers between devices, shifted(): lax.ppermute(cells, axis, [(i, (i + 1) % count) for i in range(count)])  9.53 us
    all_to_all x2, waiting for transfers between devices, per_device(): lax.all_to_all(field, 'gy', split_axis=1, concat_axis=0, tiled=True)  8.01 us
    all_to_all x2, starting transfers between devices, per_device(): lax.all_to_all(field, 'gy', split_axis=1, concat_axis=0, tiled=True)  6.94 us
  transfers between devices with their start and end apart: 12, of which 7 were waited for; matrix products, arithmetic and copies ran while one was open for 17% of the time, Pallas kernels for 0%

commit v1 on v0

--- a/solution.py
+++ b/solution.py
@@ -57,7 +57,11 @@
         local = local - half_speed_part * shifted(mixed.astype(jnp.bfloat16), "gx")
         known.append(local.astype(jnp.bfloat16))
     known = [
-        lax.all_to_all(field, "gy", split_axis=1, concat_axis=0, tiled=True) for field in known
+        jnp.concatenate(
+            lax.all_to_all(jnp.stack(jnp.split(field, lax.axis_size("gy"), axis=1)), "gy", 0, 0),
+            axis=0,
+        )
+        for field in known
     ]
     for m in range(3):
         rhs = known[m].astype(jnp.float32)

time: 145 us -> 131 us (0.903)
  the two profiles are of different devices: /device:TPU:3 before, /device:TPU:0 now
where the time goes in v1:
time: 131 us
  waiting for transfers between devices  48.6 us (37%)
  starting transfers between devices  26.3 us (20%)
  blocking collectives  19.5 us (15%)
  other arithmetic  16.9 us (13%)
  matrix products  13.8 us (11%)
  local copies, waits for them, and re-layouts  5.68 us (4%)
    ppermute x5, waiting for transfers between devices, shifted(): lax.ppermute(cells, axis, [(i, (i + 1) % count) for i in range(count)])  34.1 us
    all_to_all x1, blocking collectives, per_device(): lax.all_to_all(current.astype(jnp.bfloat16), 'gy', split_axis=0, concat_a...  19.5 us
    dot_general x3, matrix products, per_device(): current = jnp.dot(synthesis, scaled, preferred_element_type=jnp.float32)  13.8 us
    all_to_all x3, waiting for transfers between devices, per_device(): lax.all_to_all(jnp.stack(jnp.split(field, lax.axis_size('gy'), axis=1)),...  12.8 us
    all_to_all x3, starting transfers between devices, per_device(): lax.all_to_all(jnp.stack(jnp.split(field, lax.axis_size('gy'), axis=1)),...  12.1 us
    ppermute x5, starting transfers between devices, shifted(): lax.ppermute(cells, axis, [((i + 1) % count, i) for i in range(count)])  10.3 us
    convert_element_type x2, other arithmetic, per_device(): local = local - half_speed_part * shifted(mixed.astype(jnp.bfloat16), 'gx')  6.69 us
    convert_element_type x2, other arithmetic, per_device(): known.append(local.astype(jnp.bfloat16))  5.29 us
  transfers between devices with their start and end apart: 13, of which 8 were waited for; matrix products, arithmetic and copies ran while one was open for 17% of the time, Pallas kernels for 0%

profile of v1, /device:TPU:0, one launch (start us, length us, event | category | flops | bytes accessed | tf_op | source)
XLA Modules:
  0.0 130.9 jit_solution(2550933628894934486)
XLA Ops:
  0.0 0.0 copy-start
  0.0 2.9 %fusion.82 = bf16[256,1024]{1,0:T(8,128)(2,1)} fusion(bf16[4,1,256,1024]{3,2,1,0:T(8,128)(2,1)} %param.8), kind=kLoop, calls=%fused_computation.127 | loop fusion | flops 3145728 | bytes 2621440 | tf_op jit(solution)/shard_map/convert_element_type | solution.py:57
  2.9 0.5 collective-permute-start.5
  3.4 2.9 %collective-permute-start.4 = (bf16[256,1024]{1,0:T(8,128)(2,1)}, bf16[256,1024]{1,0:T(8,128)(2,1)S(1)}, u32[]{:S(2)}, u32[]{:S(2)}) collective-permute-start(bf16[256,1024]{1,0:T(8,128)(2,1)} %fusion.82), channel_id=1, source_target_pairs={{4,0},{8,4},{12,8},{16,12},{20,16},{24,20},{28,24},{0,28},{5,1},{9... | collective-permute-start | bytes 1572872 | tf_op jit(solution)/shard_map/ppermute | solution.py:30
  6.3 10.0 %collective-permute-done.5 = bf16[256,1024]{1,0:T(8,128)(2,1)S(1)} collective-permute-done((bf16[256,1024]{1,0:T(8,128)(2,1)}, bf16[256,1024]{1,0:T(8,128)(2,1)S(1)}, u32[]{:S(2)}, u32[]{:S(2)}) %collective-permute-start.5) | collective-permute-done | bytes 524320 | tf_op jit(solution)/shard_map/ppermute | solution.py:29
  16.3 1.6 %collective-permute-done.4 = bf16[256,1024]{1,0:T(8,128)(2,1)S(1)} collective-permute-done((bf16[256,1024]{1,0:T(8,128)(2,1)}, bf16[256,1024]{1,0:T(8,128)(2,1)S(1)}, u32[]{:S(2)}, u32[]{:S(2)}) %collective-permute-start.4) | collective-permute-done | bytes 524320 | tf_op jit(solution)/shard_map/ppermute | solution.py:30
  17.9 3.8 %fusion.84 = (bf16[256,1024]{1,0:T(8,128)(2,1)S(1)}, bf16[256,1024]{1,0:T(8,128)(2,1)S(1)}) fusion(bf16[4,1,256,1024]{3,2,1,0:T(8,128)(2,1)} %param.8, bf16[256,1024]{1,0:T(8,128)(2,1)S(1)} %collective-permute-done.5, bf16[256,1024]{1,0:T(8,128)(2,1)S(1)} %collective-permute-done.4, f32[256]{0:T(256)S(1)} %bitcast.213, f32[256]{0:T(256)S(1)} %bitcast.216, ...), kind=kLoop, calls=%fused_computation.129 | loop fusion | flops 10223616 | bytes 6293504 | tf_op jit(solution)/shard_map/convert_element_type | solution.py:57
  21.7 1.7 %collective-permute-start.1 = (bf16[256,1024]{1,0:T(8,128)(2,1)S(1)}, bf16[256,1024]{1,0:T(8,128)(2,1)S(1)}, u32[]{:S(2)}, u32[]{:S(2)}) collective-permute-start(bf16[256,1024]{1,0:T(8,128)(2,1)S(1)} %get-tuple-element.7), channel_id=1, source_target_pairs={{0,4},{4,8},{8,12},{12,16},{16,20},{20,24},{24,28},{28,0},{1,5},{5... | collective-permute-start | bytes 1572872 | tf_op jit(solution)/shard_map/ppermute | solution.py:29
  23.4 1.1 collective-permute-start
  24.5 11.6 %collective-permute-done.1 = bf16[256,1024]{1,0:T(8,128)(2,1)S(1)} collective-permute-done((bf16[256,1024]{1,0:T(8,128)(2,1)S(1)}, bf16[256,1024]{1,0:T(8,128)(2,1)S(1)}, u32[]{:S(2)}, u32[]{:S(2)}) %collective-permute-start.1) | collective-permute-done | bytes 524320 | tf_op jit(solution)/shard_map/ppermute | solution.py:29
  36.1 0.0 collective-permute-done
  36.1 0.0 copy-done.1
  36.1 1.5 %fusion.17 = (bf16[256,1024]{1,0:T(8,128)(2,1)S(1)}, bf16[256,1024]{1,0:T(8,128)(2,1)S(1)}) fusion(bf16[256,1024]{1,0:T(8,128)(2,1)S(1)} %collective-permute-done.1, bf16[256,1024]{1,0:T(8,128)(2,1)S(1)} %collective-permute-done, f32[256]{0:T(256)S(1)} %bitcast.214, f32[256]{0:T(256)S(1)} %bitcast.217, bf16[4,1,256,1024]{3,2,1,0:T(8,128)(2,1)S(1)} %copy-done.2, ...), kind=kLoop, calls=%fused_computation.49 | loop fusion | flops 9961472 | bytes 6293504 | tf_op jit(solution)/shard_map/convert_element_type | solution.py:58
  37.6 1.6 %collective-permute-start.3 = (bf16[256,1024]{1,0:T(8,128)(2,1)S(1)}, bf16[256,1024]{1,0:T(8,128)(2,1)}, u32[]{:S(2)}, u32[]{:S(2)}) collective-permute-start(bf16[256,1024]{1,0:T(8,128)(2,1)S(1)} %get-tuple-element.6), channel_id=1, source_target_pairs={{0,4},{4,8},{8,12},{12,16},{16,20},{20,24},{24,28},{28,0},{1,5},{5... | collective-permute-start | bytes 1572872 | tf_op jit(solution)/shard_map/ppermute | solution.py:29
  39.3 1.1 collective-permute-start.2
  40.4 0.9 pad_maximum_fusion.2
  41.2 4.5 %all-to-all-start.2 = ((bf16[4,256,256]{2,1,0:T(8,128)(2,1)}), bf16[4,256,256]{2,1,0:T(8,128)(2,1)}, u32[]{:S(2)}, u32[]{:S(2)}) async-start(bf16[4,256,256]{2,1,0:T(8,128)(2,1)} %pad_maximum_fusion.2), calls=%async_computation.2 | async-start | bytes 1048576 | tf_op jit(solution)/shard_map/all_to_all | solution.py:61
  45.7 0.8 dynamic_slice.11
  46.5 6.1 %collective-permute-done.3 = bf16[256,1024]{1,0:T(8,128)(2,1)} collective-permute-done((bf16[256,1024]{1,0:T(8,128)(2,1)S(1)}, bf16[256,1024]{1,0:T(8,128)(2,1)}, u32[]{:S(2)}, u32[]{:S(2)}) %collective-permute-start.3) | collective-permute-done | bytes 524320 | tf_op jit(solution)/shard_map/ppermute | solution.py:29
  52.6 0.0 collective-permute-done.2
  52.6 3.8 %fusion.24 = bf16[256,1024]{1,0:T(8,128)(2,1)S(1)} fusion(bf16[256,1024]{1,0:T(8,128)(2,1)} %collective-permute-done.3, bf16[256,1024]{1,0:T(8,128)(2,1)} %collective-permute-done.2, f32[256]{0:T(256)S(1)} %bitcast.215, f32[256]{0:T(256)S(1)} %bitcast.218, bf16[4,1,256,1024]{3,2,1,0:T(8,128)(2,1)} %param.9, bf16[4,1,256,1024]{3,2,1,0:T(8,128)(2,1)} %param.8), kind=kLoop, calls=%fused_computation.56 | loop fusion | flops 7864320 | bytes 5769216 | tf_op jit(solution)/shard_map/convert_element_type | solution.py:58
  56.4 0.0 copy-start.6
  56.4 0.9 pad_maximum_fusion.1
  57.3 3.0 %all-to-all-done.2 = bf16[4,256,256]{2,1,0:T(8,128)(2,1)} async-done(((bf16[4,256,256]{2,1,0:T(8,128)(2,1)}), bf16[4,256,256]{2,1,0:T(8,128)(2,1)}, u32[]{:S(2)}, u32[]{:S(2)}) %all-to-all-start.2) | async-done | bytes 524320 | tf_op jit(solution)/shard_map/all_to_all | solution.py:61
  60.3 3.5 %all-to-all-start.1 = ((bf16[4,256,256]{2,1,0:T(8,128)(2,1)}), bf16[4,256,256]{2,1,0:T(8,128)(2,1)S(1)}, u32[]{:S(2)}, u32[]{:S(2)}) async-start(bf16[4,256,256]{2,1,0:T(8,128)(2,1)} %pad_maximum_fusion.1), calls=%async_computation.1 | async-start | bytes 1048576 | tf_op jit(solution)/shard_map/all_to_all | solution.py:61
  63.8 4.4 %fusion.85 = (bf16[1024,256]{0,1:T(8,128)(2,1)}, f32[1024,256]{0,1:T(8,128)}) fusion(bf16[1024,1024]{1,0:T(8,128)(2,1)S(1)} %copy-done, bf16[1024,256]{1,0:T(8,128)(2,1)} %bitcast.30, bf16[1024,1024]{1,0:T(8,128)(2,1)} %param.14, f32[256]{0:T(256)S(1)} %dynamic_slice.11, f32[1024]{0:T(1024)S(1)} %copy-done.6), kind=kOutput, calls=%fused_computation.130 | convolution fusion | flops 1075576832 | bytes 6296576 | tf_op jit(solution)/shard_map/dot_general | solution.py:80
  68.2 0.0 collective-permute-start.7
  68.2 2.6 %collective-permute-start.6 = (bf16[1024,256]{0,1:T(8,128)(2,1)}, bf16[1024,256]{0,1:T(8,128)(2,1)}, u32[]{:S(2)}, u32[]{:S(2)}) collective-permute-start(bf16[1024,256]{0,1:T(8,128)(2,1)} %get-tuple-element.21), channel_id=1, source_target_pairs={{4,0},{8,4},{12,8},{16,12},{20,16},{24,20},{28,24},{0,28},{5,1},{9... | collective-permute-start | bytes 1572872 | tf_op jit(solution)/shard_map/ppermute | solution.py:30
  70.8 0.9 pad_maximum_fusion
  71.7 6.0 %all-to-all-done.1 = bf16[4,256,256]{2,1,0:T(8,128)(2,1)S(1)} async-done(((bf16[4,256,256]{2,1,0:T(8,128)(2,1)}), bf16[4,256,256]{2,1,0:T(8,128)(2,1)S(1)}, u32[]{:S(2)}, u32[]{:S(2)}) %all-to-all-start.1) | async-done | bytes 524320 | tf_op jit(solution)/shard_map/all_to_all | solution.py:61
  77.7 0.8 copy-done.3
  78.6 4.1 %all-to-all-start = ((bf16[4,256,256]{2,1,0:T(8,128)(2,1)}), bf16[4,256,256]{2,1,0:T(8,128)(2,1)}, u32[]{:S(2)}, u32[]{:S(2)}) async-start(bf16[4,256,256]{2,1,0:T(8,128)(2,1)} %pad_maximum_fusion), calls=%async_computation | async-start | bytes 1048576 | tf_op jit(solution)/shard_map/all_to_all | solution.py:61
  82.7 1.1 bitcast_convert_fusion
  83.8 1.3 copy.17
  85.1 0.0 collective-permute-done.7
  85.1 0.0 collective-permute-done.6
  85.2 5.3 %fusion.86 = (bf16[1024,256]{0,1:T(8,128)(2,1)}, f32[1024,256]{0,1:T(8,128)}) fusion(bf16[1024,1024]{1,0:T(8,128)(2,1)S(1)} %copy-done, bf16[1024,1024]{1,0:T(8,128)(2,1)} %param.14, bf16[1024,256]{0,1:T(8,128)(2,1)} %collective-permute-done.7, bf16[1024,256]{0,1:T(8,128)(2,1)} %collective-permute-done.6, bf16[1024,256]{0,1:T(8,128)(2,1)} %get-tuple-element.21, ...), kind=kOutput, calls=%fused_computation.131 | convolution fusion | flops 1078460416 | bytes 9450496 | tf_op jit(solution)/shard_map/dot_general | solution.py:80
  90.4 0.0 collective-permute-start.9
  90.4 2.6 %collective-permute-start.8 = (bf16[1024,256]{0,1:T(8,128)(2,1)}, bf16[1024,256]{0,1:T(8,128)(2,1)}, u32[]{:S(2)}, u32[]{:S(2)}) collective-permute-start(bf16[1024,256]{0,1:T(8,128)(2,1)} %get-tuple-element.23), channel_id=1, source_target_pairs={{4,0},{8,4},{12,8},{16,12},{20,16},{24,20},{28,24},{0,28},{5,1},{9... | collective-permute-start | bytes 1572872 | tf_op jit(solution)/shard_map/ppermute | solution.py:30
  93.1 3.8 %all-to-all-done = bf16[4,256,256]{2,1,0:T(8,128)(2,1)} async-done(((bf16[4,256,256]{2,1,0:T(8,128)(2,1)}), bf16[4,256,256]{2,1,0:T(8,128)(2,1)}, u32[]{:S(2)}, u32[]{:S(2)}) %all-to-all-start) | async-done | bytes 524320 | tf_op jit(solution)/shard_map/all_to_all | solution.py:61
  96.9 1.1 bitcast_convert_fusion.1
  98.0 1.3 copy.16
  99.3 6.5 %collective-permute-done.9 = bf16[1024,256]{0,1:T(8,128)(2,1)} collective-permute-done((bf16[1024,256]{0,1:T(8,128)(2,1)}, bf16[1024,256]{0,1:T(8,128)(2,1)}, u32[]{:S(2)}, u32[]{:S(2)}) %collective-permute-start.9) | collective-permute-done | bytes 524320 | tf_op jit(solution)/shard_map/ppermute | solution.py:29
  105.8 0.0 collective-permute-done.8
  105.8 4.1 %convolution_convert_fusion = bf16[256,1024]{1,0:T(8,128)(2,1)S(1)} fusion(bf16[1024,1024]{1,0:T(8,128)(2,1)S(1)} %copy-done, bf16[1024,1024]{1,0:T(8,128)(2,1)} %param.14, bf16[1024,256]{0,1:T(8,128)(2,1)} %collective-permute-done.9, bf16[1024,256]{0,1:T(8,128)(2,1)} %collective-permute-done.8, bf16[1024,256]{0,1:T(8,128)(2,1)} %get-tuple-element.23, ...), kind=kOutput, calls=%fused_computation.35 | convolution fusion | flops 1078460416 | bytes 8401920 | tf_op jit(solution)/shard_map/dot_general | solution.py:80
  110.0 19.5 %all_to_all.28 = bf16[4,256,256]{1,2,0:T(8,128)(2,1)S(1)} all-to-all(bf16[4,256,256]{1,2,0:T(8,128)(2,1)S(1)} %bitcast.211), channel_id=1, replica_groups=mesh['gx'=8,'gy'=4] {'gy'}, dimensions={0} | all-to-all | bytes 1048576 | tf_op jit(solution)/shard_map/all_to_all | solution.py:81
  129.5 0.1 convert_element_type.192
  129.6 1.3 copy.15
  (16 shorter events, 0.2 us)
Async XLA Ops:
  0.0 63.8 %copy-start = (bf16[1024,1024]{1,0:T(8,128)(2,1)S(1)}, bf16[1024,1024]{1,0:T(8,128)(2,1)}, u32[]{:S(2)}) copy-start(bf16[1024,1024]{1,0:T(8,128)(2,1)} %param.15) | copy-start | bytes 6291460
  0.0 6.2 %copy-start.4 = (f32[1,1024]{1,0:T(1,128)S(1)}, f32[1,1024]{1,0:T(1,128)}, u32[]{:S(2)}) copy-start(f32[1,1024]{1,0:T(1,128)} %param.10) | copy-start | bytes 12292
  0.0 6.2 %copy-start.5 = (f32[1,1024]{1,0:T(1,128)S(1)}, f32[1,1024]{1,0:T(1,128)}, u32[]{:S(2)}) copy-start(f32[1,1024]{1,0:T(1,128)} %param.11) | copy-start | bytes 12292
  2.9 13.4 %collective-permute-start.5 = (bf16[256,1024]{1,0:T(8,128)(2,1)}, bf16[256,1024]{1,0:T(8,128)(2,1)S(1)}, u32[]{:S(2)}, u32[]{:S(2)}) collective-permute-start(bf16[256,1024]{1,0:T(8,128)(2,1)} %fusion.82), channel_id=1, source_target_pairs={{0,4},{4,8},{8,12},{12,16},{16,20},{20,24},{24,28},{28,0},{1,5},{5... | collective-permute-start | bytes 1572872 | tf_op jit(solution)/shard_map/ppermute | solution.py:29
  3.4 14.5 %collective-permute-start.4 = (bf16[256,1024]{1,0:T(8,128)(2,1)}, bf16[256,1024]{1,0:T(8,128)(2,1)S(1)}, u32[]{:S(2)}, u32[]{:S(2)}) collective-permute-start(bf16[256,1024]{1,0:T(8,128)(2,1)} %fusion.82), channel_id=1, source_target_pairs={{4,0},{8,4},{12,8},{16,12},{20,16},{24,20},{28,24},{0,28},{5,1},{9... | collective-permute-start | bytes 1572872 | tf_op jit(solution)/shard_map/ppermute | solution.py:30
  17.9 18.2 %copy-start.1 = (bf16[4,1,256,1024]{3,2,1,0:T(8,128)(2,1)S(1)}, bf16[4,1,256,1024]{3,2,1,0:T(8,128)(2,1)}, u32[]{:S(2)}) copy-start(bf16[4,1,256,1024]{3,2,1,0:T(8,128)(2,1)} %param.8) | copy-start | bytes 6291460
  17.9 18.2 %copy-start.2 = (bf16[4,1,256,1024]{3,2,1,0:T(8,128)(2,1)S(1)}, bf16[4,1,256,1024]{3,2,1,0:T(8,128)(2,1)}, u32[]{:S(2)}) copy-start(bf16[4,1,256,1024]{3,2,1,0:T(8,128)(2,1)} %param.9) | copy-start | bytes 6291460
  21.7 14.4 %collective-permute-start.1 = (bf16[256,1024]{1,0:T(8,128)(2,1)S(1)}, bf16[256,1024]{1,0:T(8,128)(2,1)S(1)}, u32[]{:S(2)}, u32[]{:S(2)}) collective-permute-start(bf16[256,1024]{1,0:T(8,128)(2,1)S(1)} %get-tuple-element.7), channel_id=1, source_target_pairs={{0,4},{4,8},{8,12},{12,16},{16,20},{20,24},{24,28},{28,0},{1,5},{5... | collective-permute-start | bytes 1572872 | tf_op jit(solution)/shard_map/ppermute | solution.py:29
  23.4 12.7 %collective-permute-start = (bf16[256,1024]{1,0:T(8,128)(2,1)S(1)}, bf16[256,1024]{1,0:T(8,128)(2,1)S(1)}, u32[]{:S(2)}, u32[]{:S(2)}) collective-permute-start(bf16[256,1024]{1,0:T(8,128)(2,1)S(1)} %get-tuple-element.7), channel_id=1, source_target_pairs={{4,0},{8,4},{12,8},{16,12},{20,16},{24,20},{28,24},{0,28},{5,1},{9... | collective-permute-start | bytes 1572872 | tf_op jit(solution)/shard_map/ppermute | solution.py:30
  37.6 15.0 %collective-permute-start.3 = (bf16[256,1024]{1,0:T(8,128)(2,1)S(1)}, bf16[256,1024]{1,0:T(8,128)(2,1)}, u32[]{:S(2)}, u32[]{:S(2)}) collective-permute-start(bf16[256,1024]{1,0:T(8,128)(2,1)S(1)} %get-tuple-element.6), channel_id=1, source_target_pairs={{0,4},{4,8},{8,12},{12,16},{16,20},{20,24},{24,28},{28,0},{1,5},{5... | collective-permute-start | bytes 1572872 | tf_op jit(solution)/shard_map/ppermute | solution.py:29
  39.3 13.3 %collective-permute-start.2 = (bf16[256,1024]{1,0:T(8,128)(2,1)S(1)}, bf16[256,1024]{1,0:T(8,128)(2,1)}, u32[]{:S(2)}, u32[]{:S(2)}) collective-permute-start(bf16[256,1024]{1,0:T(8,128)(2,1)S(1)} %get-tuple-element.6), channel_id=1, source_target_pairs={{4,0},{8,4},{12,8},{16,12},{20,16},{24,20},{28,24},{0,28},{5,1},{9... | collective-permute-start | bytes 1572872 | tf_op jit(solution)/shard_map/ppermute | solution.py:30
  41.2 19.1 %all-to-all-start.2 = ((bf16[4,256,256]{2,1,0:T(8,128)(2,1)}), bf16[4,256,256]{2,1,0:T(8,128)(2,1)}, u32[]{:S(2)}, u32[]{:S(2)}) async-start(bf16[4,256,256]{2,1,0:T(8,128)(2,1)} %pad_maximum_fusion.2), calls=%async_computation.2 | async-start | bytes 1048576 | tf_op jit(solution)/shard_map/all_to_all | solution.py:61
  56.4 7.4 %copy-start.6 = (f32[1024]{0:T(1024)S(1)}, f32[1024]{0:T(1024)}, u32[]{:S(2)}) copy-start(f32[1024]{0:T(1024)} %param.12) | copy-start | bytes 12292
  60.3 17.4 %all-to-all-start.1 = ((bf16[4,256,256]{2,1,0:T(8,128)(2,1)}), bf16[4,256,256]{2,1,0:T(8,128)(2,1)S(1)}, u32[]{:S(2)}, u32[]{:S(2)}) async-start(bf16[4,256,256]{2,1,0:T(8,128)(2,1)} %pad_maximum_fusion.1), calls=%async_computation.1 | async-start | bytes 1048576 | tf_op jit(solution)/shard_map/all_to_all | solution.py:61
  68.2 17.0 %collective-permute-start.7 = (bf16[1024,256]{0,1:T(8,128)(2,1)}, bf16[1024,256]{0,1:T(8,128)(2,1)}, u32[]{:S(2)}, u32[]{:S(2)}) collective-permute-start(bf16[1024,256]{0,1:T(8,128)(2,1)} %get-tuple-element.21), channel_id=1, source_target_pairs={{0,4},{4,8},{8,12},{12,16},{16,20},{20,24},{24,28},{28,0},{1,5},{5... | collective-permute-start | bytes 1572872 | tf_op jit(solution)/shard_map/ppermute | solution.py:29
  68.2 17.0 %collective-permute-start.6 = (bf16[1024,256]{0,1:T(8,128)(2,1)}, bf16[1024,256]{0,1:T(8,128)(2,1)}, u32[]{:S(2)}, u32[]{:S(2)}) collective-permute-start(bf16[1024,256]{0,1:T(8,128)(2,1)} %get-tuple-element.21), channel_id=1, source_target_pairs={{4,0},{8,4},{12,8},{16,12},{20,16},{24,20},{28,24},{0,28},{5,1},{9... | collective-permute-start | bytes 1572872 | tf_op jit(solution)/shard_map/ppermute | solution.py:30
  77.7 0.8 copy-start.3
  78.6 18.3 %all-to-all-start = ((bf16[4,256,256]{2,1,0:T(8,128)(2,1)}), bf16[4,256,256]{2,1,0:T(8,128)(2,1)}, u32[]{:S(2)}, u32[]{:S(2)}) async-start(bf16[4,256,256]{2,1,0:T(8,128)(2,1)} %pad_maximum_fusion), calls=%async_computation | async-start | bytes 1048576 | tf_op jit(solution)/shard_map/all_to_all | solution.py:61
  90.4 15.3 %collective-permute-start.9 = (bf16[1024,256]{0,1:T(8,128)(2,1)}, bf16[1024,256]{0,1:T(8,128)(2,1)}, u32[]{:S(2)}, u32[]{:S(2)}) collective-permute-start(bf16[1024,256]{0,1:T(8,128)(2,1)} %get-tuple-element.23), channel_id=1, source_target_pairs={{0,4},{4,8},{8,12},{12,16},{16,20},{20,24},{24,28},{28,0},{1,5},{5... | collective-permute-start | bytes 1572872 | tf_op jit(solution)/shard_map/ppermute | solution.py:29
  90.4 15.3 %collective-permute-start.8 = (bf16[1024,256]{0,1:T(8,128)(2,1)}, bf16[1024,256]{0,1:T(8,128)(2,1)}, u32[]{:S(2)}, u32[]{:S(2)}) collective-permute-start(bf16[1024,256]{0,1:T(8,128)(2,1)} %get-tuple-element.23), channel_id=1, source_target_pairs={{4,0},{8,4},{12,8},{16,12},{20,16},{24,20},{28,24},{0,28},{5,1},{9... | collective-permute-start | bytes 1572872 | tf_op jit(solution)/shard_map/ppermute | solution.py:30
